TPU v7x, 768 devices: a whole 4x8x12 slice. The times are simulated.
768 devices in a mesh: row: 16 (over x_hi, y), col: 48 (over z, x_lo, core).
Axes of the slice: x: 4 (x_hi: 2, x_lo: 2; x = x_hi * 2 + x_lo), y: 8, z: 12, core: 2. Of those that a mesh axis runs over, the one named last changes fastest.
Arguments:
- features: float32 [98304, 256], P(('row', 'col')), may hold values from -6 to 6
- weight: float32 [256, 256], replicated, may hold values from -0.375 to 0.375
- cotangent: float32 [98304, 256], P(('row', 'col')), may hold values from -6 to 6
- tiles: float32 [16, 48, 16, 128, 128], P('row', 'col'), may hold values from -0.1875 to 0.1875
- tile_rows: int32 [16, 48, 16], P('row', 'col'), may hold values from -1 to 47, as said below
- tile_cols: int32 [16, 48, 16], P('row', 'col'), may hold values from 0 to 15, as said below
Outputs:
- hidden: float32 [98304, 256], P(('row', 'col'))
- grad_features: float32 [98304, 256], P(('row', 'col'))
- grad_weight: float32 [256, 256], replicated
Inputs may be any that keep to these rules, and one draw needn't show every extreme that they name: `tile_rows`: -1 marks an empty slot; otherwise a block row of the slot's row group. Live slots come first on every device, the first slot of every device is live, and some device has all 16 slots live. Several slots may share a block row or a whole position, and a block row may have no tile. `tile_cols`: A block column of the column group may be absent from a device's live slots.
All inputs are finite; a program needn't handle non-finite values.
Results may differ from a plain program's by a relative error of at most 0.0003.
Values sent between devices are 32-bit elements; how exact they have to be, the bound alone decides.
A program may use at most 32 MiB of HBM per device.

v0:
```python
import jax
import jax.numpy as jnp
from jax import lax
from jax.sharding import PartitionSpec as P

HIGHEST = lax.Precision.HIGHEST


def one_hot_of(indices, length):
    return (indices[:, None] == jnp.arange(length, dtype=jnp.int32)[None, :]).astype(jnp.float32)


def on_device(features, weight, cotangent, tiles, tile_rows, tile_cols):
    n_rowaxis = lax.axis_size("row")
    n_colaxis = lax.axis_size("col")
    node_count = features.shape[0]
    width = features.shape[1]
    block_size = tiles.shape[-1]
    block_rows = n_colaxis * node_count // block_size
    block_cols = n_rowaxis * node_count // block_size
    tile_values = tiles[0, 0]
    slot_rows = tile_rows[0, 0]
    slot_cols = tile_cols[0, 0]
    row_select = one_hot_of(slot_rows, block_rows)
    col_select = one_hot_of(slot_cols, block_cols)
    column = lax.all_gather(features, "row", axis=0, tiled=True)
    blocks = jnp.einsum(
        "sk,kif->sif", col_select, column.reshape(block_cols, block_size, width), precision=HIGHEST
    )
    forward_products = jnp.einsum("sij,sjf->sif", tile_values, blocks, precision=HIGHEST)
    partial_rows = jnp.einsum("sb,sif->bif", row_select, forward_products, precision=HIGHEST)
    partial_rows = partial_rows.reshape(block_rows * block_size, width)
    aggregated = lax.psum_scatter(partial_rows, "col", scatter_dimension=0, tiled=True)
    preact = jnp.dot(aggregated, weight, precision=HIGHEST)
    hidden = jnp.tanh(preact)
    delta_pre = cotangent * (1.0 - hidden * hidden)
    grad_weight = lax.psum(jnp.dot(aggregated.T, delta_pre, precision=HIGHEST), ("row", "col"))
    back_rows = jnp.dot(delta_pre, weight.T, precision=HIGHEST)
    row_group = lax.all_gather(back_rows, "col", axis=0, tiled=True)
    picked = jnp.einsum(
        "sb,bif->sif",
        row_select,
        row_group.reshape(block_rows, block_size, width),
        precision=HIGHEST,
    )
    backward_products = jnp.einsum("sji,sjf->sif", tile_values, picked, precision=HIGHEST)
    partial_cols = jnp.einsum("sk,sif->kif", col_select, backward_products, precision=HIGHEST)
    partial_cols = partial_cols.reshape(block_cols * block_size, width)
    grad_features = lax.psum_scatter(partial_cols, "row", scatter_dimension=0, tiled=True)
    return (hidden, grad_features, grad_weight)


def solution(mesh):
    placed = (
        P(("row", "col"), None),
        P(),
        P(("row", "col"), None),
        P("row", "col", None, None, None),
        P("row", "col", None),
        P("row", "col", None),
    )
    return jax.shard_map(
        on_device,
        mesh=mesh,
        in_specs=placed,
        out_specs=(P(("row", "col"), None), P(("row", "col"), None), P()),
        check_vma=False,
    )
```

profile of v0, /device:TPU:1, one launch (start us, length us, event | category | flops | bytes accessed | tf_op | source)
XLA Modules:
  0.0 1109.6 jit_solution(8809615139788986324)
XLA Ops:
  7.2 0.0 copy-start
  7.2 0.0 all-gather.3.cloned.1.call-start
  7.2 0.7 all-gather.3.cloned.1.call-update
  7.9 0.0 reduce-scatter.3.cloned.1.call-start
  8.0 104.1 %all-gather.3.cloned.1.call-done = f32[2048,256]{1,0:T(8,128)} async-done(((f32[128,256]{1,0:T(8,128)}), f32[2048,256]{1,0:T(8,128)}) %all-gather.3.cloned.1.call-update) | async-done | bytes 2097168 | tf_op jit(solution)/shard_map/all_gather | solution.py:26
  112.1 3.8 fusion.10
  115.9 0.0 copy-done
  115.9 4.6 fusion.8
  120.5 0.0 copy-start.4
  120.5 2.2 copy.13
  122.8 0.0 copy-done.4
  122.8 4.3 fusion.4
  127.1 6.3 copy.9
  133.4 0.0 copy-start.2
  133.4 0.0 copy-start.3
  133.4 0.0 reduce-scatter.3.cloned.1.call-update
  133.4 0.0 all-gather.5.cloned.1.call-start
  133.5 183.1 %reduce-scatter.3.cloned.1.call-done = f32[128,256]{1,0:T(8,128)} async-done(((f32[6144,256]{1,0:T(8,128)}), f32[128,256]{1,0:T(8,128)}) %reduce-scatter.3.cloned.1.call-update) | async-done | bytes 131088 | tf_op jit(solution)/shard_map/reduce_scatter | solution.py:33
  316.6 0.0 copy-done.2
  316.6 1.2 convolution_tanh_fusion
  317.8 0.0 copy-done.3
  317.8 0.0 copy-start.1
  317.8 1.1 fusion.15
  318.8 0.0 all-gather.5.cloned.1.call-update
  318.9 0.0 all-reduce.2.cloned.1.call-start
  318.9 2.0 fusion.14
  320.9 0.0 all-reduce.2.cloned.1.call-update
  321.0 0.0 reduce-scatter.5.cloned.1.call-start
  321.0 101.0 %all-gather.5.cloned.1.call-done = f32[6144,256]{1,0:T(8,128)} async-done(((f32[128,256]{1,0:T(8,128)}), f32[6144,256]{1,0:T(8,128)}) %all-gather.5.cloned.1.call-update) | async-done | bytes 6291472 | tf_op jit(solution)/shard_map/all_gather | solution.py:39
  422.0 8.4 fusion
  430.4 0.0 copy-done.1
  430.4 4.6 fusion.6
  435.0 0.0 copy-start.5
  435.0 2.1 copy.16
  437.1 0.0 copy-done.5
  437.1 2.7 fusion.2
  439.8 2.5 copy.10
  442.3 0.0 reduce-scatter.5.cloned.1.call-update
  442.3 445.1 %all-reduce.2.cloned.1.call-done = f32[256,256]{1,0:T(8,128)} async-done(((f32[256,256]{1,0:T(8,128)}), f32[256,256]{1,0:T(8,128)}) %all-reduce.2.cloned.1.call-update) | async-done | bytes 262160 | tf_op jit(solution)/shard_map/psum | solution.py:37
  887.4 214.0 %reduce-scatter.5.cloned.1.call-done = f32[128,256]{1,0:T(8,128)} async-done(((f32[2048,256]{1,0:T(8,128)}), f32[128,256]{1,0:T(8,128)}) %reduce-scatter.5.cloned.1.call-update) | async-done | bytes 131088 | tf_op jit(solution)/shard_map/reduce_scatter | solution.py:49
  1101.4 1.7 copy.26
Async XLA Ops:
  7.2 108.7 %copy-start = (f32[1,1,16,128,128]{4,3,2,1,0:T(8,128)S(1)}, f32[1,1,16,128,128]{4,3,2,1,0:T(8,128)}, u32[]{:S(2)}) copy-start(f32[1,1,16,128,128]{4,3,2,1,0:T(8,128)} %param.9) | copy-start | bytes 3145732
  7.2 104.9 %all-gather.3.cloned.1.call-start = ((), (), s32[]{:S(2)}) async-start(), calls=%async_computation.2 | async-start | bytes 2228224 | tf_op jit(solution)/shard_map/all_gather | solution.py:26
  7.9 308.6 %reduce-scatter.3.cloned.1.call-start = ((), (), s32[]{:S(2)}) async-start(), calls=%async_computation.3 | async-start | bytes 6422528 | tf_op jit(solution)/shard_map/reduce_scatter | solution.py:33
  120.5 2.2 copy-start.4
  133.4 183.2 %copy-start.2 = (f32[256,256]{1,0:T(8,128)S(1)}, f32[256,256]{1,0:T(8,128)}, u32[]{:S(2)}) copy-start(f32[256,256]{1,0:T(8,128)} %param.7) | copy-start | bytes 786436
  133.4 184.4 %copy-start.3 = (f32[128,256]{1,0:T(8,128)S(1)}, f32[128,256]{1,0:T(8,128)}, u32[]{:S(2)}) copy-start(f32[128,256]{1,0:T(8,128)} %param.8) | copy-start | bytes 393220
  133.4 288.6 %all-gather.5.cloned.1.call-start = ((), (), s32[]{:S(2)}) async-start(), calls=%async_computation.4 | async-start | bytes 6422528 | tf_op jit(solution)/shard_map/all_gather | solution.py:39
  317.8 112.6 %copy-start.1 = (f32[128,256]{1,0:T(8,128)}, f32[128,256]{1,0:T(8,128)S(1)}, u32[]{:S(2)}) copy-start(f32[128,256]{1,0:T(8,128)S(1)} %convolution_tanh_fusion) | copy-start | bytes 393220
  318.9 568.6 %all-reduce.2.cloned.1.call-start = ((), (), s32[]{:S(2)}) async-start(), calls=%async_computation.6 | async-start | bytes 524288 | tf_op jit(solution)/shard_map/psum | solution.py:37
  321.0 780.5 %reduce-scatter.5.cloned.1.call-start = ((), (), s32[]{:S(2)}) async-start(), calls=%async_computation.5 | async-start | bytes 2228224 | tf_op jit(solution)/shard_map/reduce_scatter | solution.py:49
  435.0 2.1 copy-start.5
Sparse Core Ops, SparseCore 0:
  11.8 100.2 all-gather.2
  133.5 182.9 reduce-scatter.2
  319.6 102.3 all-gather.4
  427.9 459.5 all-reduce.1
  893.7 207.6 reduce-scatter.4
where the time goes:
time: 1110 us
  waiting for transfers between devices  1050 us (95%)
  matrix products  32.7 us (3%)
  local copies, waits for them, and re-layouts  14.8 us (1%)
  between operations  13.9 us (1%)
    psum x1, waiting for transfers between devices, on_device(): lax.psum(jnp.dot(aggregated.T, delta_pre, precision=HIGHEST), ('row', 'co...  445 us
    reduce_scatter x1, waiting for transfers between devices, on_device(): lax.psum_scatter(partial_cols, 'row', scatter_dimension=0, tiled=True)  214 us
    reduce_scatter x1, waiting for transfers between devices, on_device(): lax.psum_scatter(partial_rows, 'col', scatter_dimension=0, tiled=True)  183 us
    all_gather x1, waiting for transfers between devices, on_device(): column = lax.all_gather(features, 'row', axis=0, tiled=True)  104 us
    all_gather x1, waiting for transfers between devices, on_device(): row_group = lax.all_gather(back_rows, 'col', axis=0, tiled=True)  101 us
  transfers between devices with their start and end apart: 5, of which 5 were waited for; matrix products, arithmetic and copies ran while one was open for 2% of the time, Pallas kernels for 0%

commit v1 on v0

v1 whole, which is shorter than its diff:
```python
import functools

import jax
import jax.numpy as jnp
from jax import lax
from jax.experimental import pallas as pl
from jax.experimental.pallas import tpu as pltpu
from jax.sharding import PartitionSpec as P

MESH = pl.DeviceIdType.MESH
F32 = jnp.float32
BF16 = jnp.bfloat16
BLK = 128


def split(v):
    high = v.astype(BF16)
    return high, (v - high.astype(F32)).astype(BF16)


def dot3(a, b, dims=((1,), (0,))):
    ah, al = split(a)
    bh, bl = split(b)

    def one(p, q):
        return lax.dot_general(p, q, (dims, ((), ())), preferred_element_type=F32)

    return one(ah, bh) + (one(ah, bl) + one(al, bh))


def layer_kernel(ny, nz, feat, w, cot, tiles, trows, tcols, hid, gfeat, gwo, meta_out, *scratch):
    (halves, xb, sib, meta, prod,
     zs, zr, zqs, zqr, agg, ab, ys, yr, yqs, yqr, fin,
     g0, r1, s1, r2, s2, r3, r4, s4, gout,
     sm, mloc, tq_s, tq_r,
     xq_s, xq_r, xr_s, xr_r, zrs_s, zrs_r, zq_s, zq_r,
     bq_s, bq_r, br_s, br_r, yrs_s, yrs_r, yq_s, yq_r,
     g1_s, g1_r, g2_s, g2_r, g3_s, g3_r, g4_s, g4_r, g5_s, g5_r, g6_s, g6_r) = scratch
    r = lax.axis_index("row")
    c = lax.axis_index("col")
    xh, y = r // ny, r % ny
    z, xl, k = c // 4, (c // 2) % 2, c % 2
    sgn = 1 - 2 * k
    slots = tiles.shape[0]

    def dev(xh_, y_, z_, xl_, k_):
        return (xh_ * ny + y_, z_ * 4 + xl_ * 2 + k_)

    def quad_x(q):
        return dev((xh + q // 2) % 2, y, z, xl, (k + q % 2) % 2)

    def quad_l(q):
        return dev(xh, y, z, (xl + q // 2) % 2, (k + q % 2) % 2)

    def at_y(d):
        return dev(xh, (y + d + ny) % ny, z, xl, k)

    def at_z(d):
        return dev(xh, y, (z + d + nz) % nz, xl, k)

    def remote(src, dst, ss, rs, to):
        return pltpu.make_async_remote_copy(
            src_ref=src, dst_ref=dst, send_sem=ss, recv_sem=rs, device_id=to, device_id_type=MESH)

    peers = [quad_x(1), quad_x(2), quad_x(3), quad_l(2), quad_l(3)]
    peers += [at_y(d) for d in range(1, ny)]
    peers += [at_z(d) for d in range(1, nz)]
    barrier = pltpu.get_barrier_semaphore()
    for to in peers:
        pl.semaphore_signal(barrier, inc=1, device_id=to, device_id_type=MESH)
    pl.semaphore_wait(barrier, len(peers))

    def lane_of(xbit, q):
        return ((xbit + q // 2) % 2) * 2 + (k + q % 2) % 2

    class Gather:
        def __init__(self, buf, src, pos, n, xbit, quad, ring, qs, qr, ss, rs):
            self.__dict__.update(locals())
            self.h = n // 2

        def entry(self, p, q):
            return self.buf.at[((p + 2 * self.n) % self.n) * 4 + lane_of(self.xbit, q)]

        def first(self, q):
            ref = self.entry(self.pos, 0)
            return remote(self.src.at[(k + q % 2) % 2], ref, self.qs.at[q - 1], self.qr.at[q - 1], self.quad(q))

        def first_arrival(self, q):
            ref = self.entry(self.pos, q)
            return remote(ref, ref, self.qs.at[q - 1], self.qr.at[q - 1], self.quad(q))

        def step(self, d, j, q, shift=0):
            way = sgn if d == 0 else -sgn
            ref = self.entry(self.pos - way * (j + shift), q)
            return remote(ref, ref, self.ss.at[d, j, q], self.rs.at[d, j, q], self.ring(way))

        def arrival(self, d, j, q):
            return self.step(d, j, q, 1)

        def start(self):
            for q in (1, 2, 3):
                self.first(q).start()
            idx = self.pos * 4 + lane_of(self.xbit, 0)
            self.buf[pl.ds(idx, 1)] = self.src[pl.ds(k, 1)]
            self.step(0, 0, 0).start()
            self.step(1, 0, 0).start()

        def enter(self):
            for q in (1, 2, 3):
                self.first_arrival(q).wait_recv()
                self.step(0, 0, q).start()
                self.step(1, 0, q).start()

        def forward(self, j):
            for q in range(4):
                for d in (0, 1):
                    self.arrival(d, j - 1, q).wait_recv()
                    if j < self.h - 1 or d == 0:
                        self.step(d, j, q).start()

        def finish(self):
            for q in range(4):
                self.arrival(0, self.h - 1, q).wait_recv()

        def drain(self):
            for q in (1, 2, 3):
                self.first(q).wait_send()

            def both(j, carry):
                for q in range(4):
                    for d in (0, 1):
                        self.step(d, j, q).wait_send()
                return carry

            lax.fori_loop(0, self.h - 1, both, 0)
            for q in range(4):
                self.step(0, self.h - 1, q).wait_send()

    class Scatter:
        def __init__(self, part, first, got, qsend, qgot, pos, n, xbit, quad, ring, ss, rs, qs, qr):
            self.__dict__.update(locals())
            self.h = n // 2

        def own(self, d, j, q):
            ahead = self.h - j if d == 0 else -(self.h - 1 - j)
            p = (self.pos + sgn * ahead + self.n) % self.n
            return self.part(p, lane_of(self.xbit, q))

        def step(self, d, j, q, src):
            way = sgn if d == 0 else -sgn
            return remote(src, self.got.at[d, j, q], self.ss.at[d, j, q], self.rs.at[d, j, q], self.ring(way))

        def arrival(self, d, j, q):
            return self.step(d, j, q, self.got.at[d, j, q])

        def begin(self):
            def lane(q, carry):
                for d in (0, 1):
                    self.first[d, q] = self.own(d, 0, q)
                    self.step(d, 0, q, self.first.at[d, q]).start()
                return carry

            lax.fori_loop(0, 4, lane, 0)

        def pass_on(self, d, j, q):
            value = self.own(d, j, q)
            self.arrival(d, j - 1, q).wait_recv()
            self.got[d, j - 1, q] = self.got[d, j - 1, q] + value
            self.step(d, j, q, self.got.at[d, j - 1, q]).start()

        def run(self):
            self.begin()

            def both(t, carry):
                for d in (0, 1):
                    self.pass_on(d, t // 4 + 1, t % 4)
                return carry

            lax.fori_loop(0, 4 * (self.h - 2), both, 0)

            def last(q, carry):
                self.pass_on(0, self.h - 1, q)
                return carry

            lax.fori_loop(0, 4, last, 0)

        def total(self, q):
            value = self.part(self.pos, lane_of(self.xbit, q))
            self.arrival(1, self.h - 2, q).wait_recv()
            self.arrival(0, self.h - 1, q).wait_recv()
            return value + self.got[0, self.h - 1, q] + self.got[1, self.h - 2, q]

        def handover(self, q, i):
            return remote(self.qsend.at[i], self.qgot.at[i], self.qs.at[i], self.qr.at[i], self.quad(q))

        def finish(self, out):
            for q in (1, 2, 3):
                self.qsend[q - 1] = self.total(q)
                self.handover(q, q - 1).start()
            mine = self.total(0)
            self.handover(2, 1).wait_recv()
            out[pl.ds(k, 1)] = (mine + self.qgot[1])[None]
            self.handover(1, 0).wait_recv()
            self.handover(3, 2).wait_recv()
            out[pl.ds(1 - k, 1)] = (self.qgot[0] + self.qgot[2])[None]

        def drain(self):
            for q in (1, 2, 3):
                self.handover(q, q - 1).wait_send()

            def both(t, carry):
                for d in (0, 1):
                    self.arrival(d, t // 4, t % 4).wait_send()
                return carry

            lax.fori_loop(0, 4 * (self.h - 1), both, 0)
            for q in range(4):
                self.arrival(0, self.h - 1, q).wait_send()

    halves[0] = feat[:, :BLK]
    halves[1] = feat[:, BLK:]
    column = Gather(xb, halves, y, ny, xh, quad_x, at_y, xq_s, xq_r, xr_s, xr_r)
    column.start()
    send_rows = remote(trows, meta_out.at[0], tq_s.at[1], tq_r.at[1], quad_x(1))
    send_cols = remote(tcols, meta_out.at[1], tq_s.at[2], tq_r.at[2], quad_x(1))
    send_rows.start()
    send_cols.start()
    own_rows = pltpu.make_async_copy(trows, sm.at[0], mloc.at[0])
    own_cols = pltpu.make_async_copy(tcols, sm.at[1], mloc.at[1])
    own_rows.start()
    own_cols.start()
    column.enter()
    send_tiles = remote(tiles, sib, tq_s.at[0], tq_r.at[0], quad_x(1))
    send_tiles.start()
    send_rows.wait_recv()
    send_cols.wait_recv()
    own_rows.wait()
    own_cols.wait()
    sib_rows = pltpu.make_async_copy(meta_out.at[0], sm.at[2], mloc.at[2])
    sib_cols = pltpu.make_async_copy(meta_out.at[1], sm.at[3], mloc.at[3])
    sib_rows.start()
    sib_cols.start()
    sib_rows.wait()
    sib_cols.wait()
    for j in range(1, ny // 2):
        column.forward(j)
    send_tiles.wait_recv()
    column.finish()

    tile_of = (tiles, sib)

    def row_at(g, s):
        return sm[2 * g, s]

    def col_at(g, s):
        return sm[2 * g + 1, s]

    def core_of(g):
        return (k + g) % 2

    def products(s, carry):
        for g in (0, 1):
            col = col_at(g, s)
            place = (col % ny) * 4 + (col // ny) * 2 + core_of(g)
            prod[g * slots + s] = dot3(tile_of[g][s], xb[place])
        return carry

    lax.fori_loop(0, slots, products, 0)

    def row_part(p, lane):
        block = p * 4 + lane
        acc = jnp.zeros((BLK, BLK), F32)
        for g in (0, 1):
            for s in range(slots):
                acc = acc + jnp.where(row_at(g, s) == block, 1.0, 0.0) * prod[g * slots + s]
        return acc

    rows = Scatter(row_part, zs, zr, zqs, zqr, z, nz, xl, quad_l, at_z, zrs_s, zrs_r, zq_s, zq_r)
    rows.run()
    rows.finish(agg)

    aggregated = jnp.concatenate([agg[0], agg[1]], axis=1)
    hidden = jnp.tanh(dot3(aggregated, w[...]))
    hid[...] = hidden
    delta = cot[...] * (1.0 - hidden * hidden)
    back = dot3(delta, w[...], ((1,), (1,)))
    column.drain()
    halves[0] = back[:, :BLK]
    halves[1] = back[:, BLK:]
    group = Gather(ab, halves, z, nz, xl, quad_l, at_z, bq_s, bq_r, br_s, br_r)
    group.start()

    g0[...] = dot3(aggregated, delta, ((0,), (0,))).reshape(g0.shape)
    m = lane_of(xl, 0)
    per = g0.shape[0] // ny

    def chunk(p):
        return pl.ds(((p + ny) % ny) * per, per)

    def sum_y(d):
        return remote(g0.at[chunk(y + d)], r1.at[d - 1], g1_s.at[d - 1], g1_r.at[d - 1], at_y(d))

    def sum_quad(q):
        return remote(s1.at[lane_of(xl, q)], r2.at[q - 1], g2_s.at[q - 1], g2_r.at[q - 1], quad_l(q))

    def sum_x():
        return remote(s2, r3, g3_s.at[0], g3_r.at[0], quad_x(2))

    def sum_z(d):
        return remote(s4.at[0], r4.at[z], g4_s.at[d - 1], g4_r.at[d - 1], at_z(d))

    def sum_z_in(d):
        return remote(s4.at[0], r4.at[(z - d + nz) % nz], g4_s.at[d - 1], g4_r.at[d - 1], at_z(d))

    def spread_quad(q, p):
        ref = gout.at[y * per + lane_of(xl, p)]
        return remote(ref, ref, g5_s.at[q - 1], g5_r.at[q - 1], quad_l(q))

    def spread_y(d, back_by):
        ref = gout.at[chunk(y - back_by)]
        return remote(ref, ref, g6_s.at[d - 1], g6_r.at[d - 1], at_y(d))

    for d in range(1, ny):
        sum_y(d).start()
    group.enter()

    group.forward(1)
    acc = g0[chunk(y)]
    for d in range(1, ny):
        sum_y(d).wait_recv()
        acc = acc + r1[d - 1]
    s1[...] = acc
    for q in (1, 2, 3):
        sum_quad(q).start()

    group.forward(2)
    acc = s1[m]
    for q in (1, 2, 3):
        sum_quad(q).wait_recv()
        acc = acc + r2[q - 1]
    s2[...] = acc
    sum_x().start()

    group.forward(3)
    sum_x().wait_recv()
    s4[0] = s2[...] + r3[...]
    for d in range(1, nz):
        sum_z(d).start()
    r4[z] = s4[0]

    group.forward(4)
    for d in range(1, nz):
        sum_z_in(d).wait_recv()
    acc = r4[0]
    for p in range(1, nz):
        acc = acc + r4[p]
    gout[y * per + m] = acc
    for q in (1, 2, 3):
        spread_quad(q, 0).start()

    for j in range(5, nz // 2):
        group.forward(j)
    for q in (1, 2, 3):
        spread_quad(q, q).wait_recv()
    for d in range(1, ny):
        spread_y(d, 0).start()
    group.finish()

    def back_products(s, carry):
        for g in (0, 1):
            row = jnp.maximum(row_at(g, s), 0)
            prod[g * slots + s] = dot3(tile_of[g][s], ab[row], ((0,), (0,)))
        return carry

    lax.fori_loop(0, slots, back_products, 0)

    def col_part(p, lane):
        block = (lane // 2) * ny + p
        acc = jnp.zeros((BLK, BLK), F32)
        g_base = ((lane + k) % 2) * slots
        which = (lane + k) % 2
        for s in range(slots):
            live = (sm[2 * which + 1, s] == block) & (sm[2 * which, s] >= 0)
            acc = acc + jnp.where(live, 1.0, 0.0) * prod[g_base + s]
        return acc

    cols = Scatter(col_part, ys, yr, yqs, yqr, y, ny, xh, quad_x, at_y, yrs_s, yrs_r, yq_s, yq_r)
    cols.run()
    cols.finish(fin)
    gfeat[:, :BLK] = fin[0]
    gfeat[:, BLK:] = fin[1]

    for d in range(1, ny):
        spread_y(d, d).wait_recv()
    gwo[...] = gout[...].reshape(gwo.shape)

    send_tiles.wait_send()
    send_rows.wait_send()
    send_cols.wait_send()
    group.drain()
    rows.drain()
    cols.drain()
    for d in range(1, ny):
        sum_y(d).wait_send()
        spread_y(d, 0).wait_send()
    for q in (1, 2, 3):
        sum_quad(q).wait_send()
        spread_quad(q, 0).wait_send()
    sum_x().wait_send()
    for d in range(1, nz):
        sum_z(d).wait_send()


def on_device(features, weight, cotangent, tiles, tile_rows, tile_cols):
    ny = lax.axis_size("row") // 2
    nz = lax.axis_size("col") // 4
    node_count, width = features.shape
    slots = tiles.shape[2]
    half = (BLK, BLK)
    hy, hz = ny // 2, nz // 2
    lines = width // 8
    per = lines // ny
    dma = pltpu.SemaphoreType.DMA
    vmem = pltpu.VMEM
    scratch = [
        vmem((2,) + half, F32), vmem((ny * 4,) + half, F32), vmem((slots,) + half, F32),
        vmem((8, 128), jnp.int32), vmem((2 * slots,) + half, F32),
        vmem((2, 4) + half, F32), vmem((2, hz, 4) + half, F32), vmem((3,) + half, F32), vmem((3,) + half, F32),
        vmem((2,) + half, F32), vmem((nz * 4,) + half, F32),
        vmem((2, 4) + half, F32), vmem((2, hy, 4) + half, F32), vmem((3,) + half, F32), vmem((3,) + half, F32),
        vmem((2,) + half, F32),
        vmem((lines, 8, width), F32), vmem((ny - 1, per, 8, width), F32), vmem((per, 8, width), F32),
        vmem((3, 8, width), F32), vmem((8, width), F32), vmem((8, width), F32),
        vmem((nz, 8, width), F32), vmem((1, 8, width), F32), vmem((lines, 8, width), F32),
        pltpu.SMEM((4, slots), jnp.int32), dma((4,)), dma((3,)), dma((3,)),
        dma((3,)), dma((3,)), dma((2, hy, 4)), dma((2, hy, 4)),
        dma((2, hz, 4)), dma((2, hz, 4)), dma((3,)), dma((3,)),
        dma((3,)), dma((3,)), dma((2, hz, 4)), dma((2, hz, 4)),
        dma((2, hy, 4)), dma((2, hy, 4)), dma((3,)), dma((3,)),
        dma((ny - 1,)), dma((ny - 1,)), dma((3,)), dma((3,)), dma((1,)), dma((1,)),
        dma((nz - 1,)), dma((nz - 1,)), dma((3,)), dma((3,)), dma((ny - 1,)), dma((ny - 1,)),
    ]
    in_vmem = pl.BlockSpec(memory_space=pltpu.VMEM)
    anywhere = pl.BlockSpec(memory_space=pl.ANY)
    out = pl.pallas_call(
        functools.partial(layer_kernel, ny, nz),
        out_shape=(
            jax.ShapeDtypeStruct((node_count, width), F32),
            jax.ShapeDtypeStruct((node_count, width), F32),
            jax.ShapeDtypeStruct((width, width), F32),
            jax.ShapeDtypeStruct((2, slots), jnp.int32),
        ),
        in_specs=[in_vmem] * 4 + [anywhere] * 2,
        out_specs=(in_vmem, in_vmem, in_vmem, anywhere),
        scratch_shapes=scratch,
        compiler_params=pltpu.CompilerParams(
            collective_id=0, has_side_effects=True, vmem_limit_bytes=40 * 1024 * 1024),
    )(features, weight, cotangent, tiles[0, 0], tile_rows[0, 0], tile_cols[0, 0])
    return out[0], out[1], out[2]


def solution(mesh):
    placed = (
        P(("row", "col"), None),
        P(),
        P(("row", "col"), None),
        P("row", "col", None, None, None),
        P("row", "col", None),
        P("row", "col", None),
    )
    return jax.shard_map(
        on_device,
        mesh=mesh,
        in_specs=placed,
        out_specs=(P(("row", "col"), None), P(("row", "col"), None), P()),
        check_vma=False,
    )
```

time: 1110 us -> 162 us (0.15)
  waiting for transfers between devices: 1050 us -> 0 us
  Pallas kernels: 0 us -> 155 us
  matrix products: 32.7 us -> 0 us
  between operations: 13.9 us -> 0.66 us
    psum x1 -> x0, waiting for transfers between devices: 445 us -> none  [on_device(): lax.psum(jnp.dot(aggregated.T, delta_pre, precision=HIGHEST), ('row', 'co...]
    reduce_scatter x2 -> x0, waiting for transfers between devices: 397 us -> none  [the longest x1 214 us: on_device(): lax.psum_scatter(partial_cols, 'row', scatter_dimension=0, tiled=True)]
    all_gather x2 -> x0, waiting for transfers between devices: 205 us -> none  [the longest x1 104 us: on_device(): column = lax.all_gather(features, 'row', axis=0, tiled=True)]
    pallas_call x0 -> x1, Pallas kernels: none -> 155 us  [on_device(): pl.pallas_call(functools.partial(layer_kernel, ny, nz), out_shape=(jax.Sh...]
    dot_general x9 -> x0, matrix products: 32.7 us -> none  [the longest x1 8.36 us: on_device(): jnp.einsum('sb,bif->sif', row_select, row_group.reshape(block_rows, block...]
    dot_general x4 -> x0, local copies, waits for them, and re-layouts: 13.1 us -> none  [the longest x1 6.29 us: on_device(): jnp.einsum('sb,sif->bif', row_select, forward_products, precision=HIGHEST)]
  transfers between devices with their start and end apart: 5 -> 0, of which waited for: 5 -> 0; matrix products, arithmetic and copies ran while one was open for 2% -> 0% of each run, Pallas kernels for 0% -> 0%
where the time goes in v1:
time: 162 us
  Pallas kernels  155 us (96%)
  local copies, waits for them, and re-layouts  6.65 us (4%)
    pallas_call x1, Pallas kernels, on_device(): pl.pallas_call(functools.partial(layer_kernel, ny, nz), out_shape=(jax.Sh...  155 us
    unnamed x15, local copies, waits for them, and re-layouts  6.65 us

profile of v1, /device:TPU:1, one launch (start us, length us, event | category | flops | bytes accessed | tf_op | source)
XLA Modules:
  0.0 162.0 jit_solution(9995735015432162399)
XLA Ops:
  0.6 0.0 copy-start.4
  0.6 0.0 copy-start.5
  0.7 0.6 copy-done.4
  1.3 0.0 copy-done.5
  1.3 0.0 copy-start
  1.3 1.2 copy-done
  2.5 0.0 copy-start.1
  2.5 0.9 copy-done.1
  3.5 0.0 copy-start.2
  3.5 0.9 copy-done.2
  4.4 0.0 copy-start.3
  4.4 0.9 copy-done.3
  5.3 154.7 %shard_map.85 = (f32[128,256]{1,0:T(8,128)S(1)}, f32[128,256]{1,0:T(8,128)S(1)}, f32[256,256]{1,0:T(8,128)S(1)}, s32[2,16]{1,0:T(2,128)}) custom-call(f32[128,256]{1,0:T(8,128)S(1)} %copy-done.2, f32[256,256]{1,0:T(8,128)S(1)} %copy-done.1, f32[128,256]{1,0:T(8,128)S(1)} %copy-done.3, f32[16,128,128]{2,1,0:T(8,128)S(1)} %bitcast.3, s32[16]{0:T(128)S(1)} %bitcast.4, ...), custom_call_target="tpu_custom_call" | custom-call | tf_op jit(solution)/shard_map/pallas_call | solution.py:445
  160.0 0.7 copy.12
  160.6 0.7 copy.13
  161.3 0.7 copy.14
Async XLA Ops:
  0.6 0.7 copy-start.4
  0.6 0.7 copy-start.5
  1.3 1.2 copy-start
  2.5 0.9 copy-start.1
  3.5 0.9 copy-start.2
  4.4 0.9 copy-start.3

commit v2 on v1

--- a/solution.py
+++ b/solution.py
@@ -11,6 +11,7 @@
 F32 = jnp.float32
 BF16 = jnp.bfloat16
 BLK = 128
+NEAR = 3
 
 
 def split(v):
@@ -28,14 +29,15 @@
     return one(ah, bh) + (one(ah, bl) + one(al, bh))
 
 
-def layer_kernel(ny, nz, feat, w, cot, tiles, trows, tcols, hid, gfeat, gwo, meta_out, *scratch):
-    (halves, xb, sib, meta, prod,
+def layer_kernel(ny, nz, feat, w_in, cot_in, tiles_in, trows, tcols, hid, gfeat, gwo, meta_out, *scratch):
+    (halves, w, cot, tiles, xb, sib, prod,
      zs, zr, zqs, zqr, agg, ab, ys, yr, yqs, yqr, fin,
      g0, r1, s1, r2, s2, r3, r4, s4, gout,
-     sm, mloc, tq_s, tq_r,
+     sm, mloc, tq_s, tq_r, loads,
      xq_s, xq_r, xr_s, xr_r, zrs_s, zrs_r, zq_s, zq_r,
      bq_s, bq_r, br_s, br_r, yrs_s, yrs_r, yq_s, yq_r,
-     g1_s, g1_r, g2_s, g2_r, g3_s, g3_r, g4_s, g4_r, g5_s, g5_r, g6_s, g6_r) = scratch
+     g1_s, g1_r, g2_s, g2_r, g3_s, g3_r, g4_s, g4_r, g5_s, g5_r, g6_s, g6_r,
+     hs, hr, hop_s, hop_r, bx_s, bx_r, pairs) = scratch
     r = lax.axis_index("row")
     c = lax.axis_index("col")
     xh, y = r // ny, r % ny
@@ -65,16 +67,27 @@
     peers = [quad_x(1), quad_x(2), quad_x(3), quad_l(2), quad_l(3)]
     peers += [at_y(d) for d in range(1, ny)]
     peers += [at_z(d) for d in range(1, nz)]
+    load = [pltpu.make_async_copy(src, dst, loads.at[i]) for i, (src, dst) in enumerate((
+        (feat.at[:, pl.ds(0, BLK)], halves.at[0]), (feat.at[:, pl.ds(BLK, BLK)], halves.at[1]),
+        (tiles_in, tiles), (w_in, w), (cot_in, cot)))]
     barrier = pltpu.get_barrier_semaphore()
     for to in peers:
         pl.semaphore_signal(barrier, inc=1, device_id=to, device_id_type=MESH)
+    for item in load:
+        item.start()
+    own_rows = pltpu.make_async_copy(trows, sm.at[0], mloc.at[0])
+    own_cols = pltpu.make_async_copy(tcols, sm.at[1], mloc.at[1])
+    own_rows.start()
+    own_cols.start()
+    load[0].wait()
+    load[1].wait()
     pl.semaphore_wait(barrier, len(peers))
 
     def lane_of(xbit, q):
         return ((xbit + q // 2) % 2) * 2 + (k + q % 2) % 2
 
     class Gather:
-        def __init__(self, buf, src, pos, n, xbit, quad, ring, qs, qr, ss, rs):
+        def __init__(self, buf, src, pos, n, xbit, quad, ring, qs, qr, ss, rs, near=0, xs=None, xr=None):
             self.__dict__.update(locals())
             self.h = n // 2
 
@@ -97,30 +110,49 @@
         def arrival(self, d, j, q):
             return self.step(d, j, q, 1)
 
+        def relay(self, d, i, q, other=0):
+            way = sgn if d == 0 else -sgn
+            ref = self.entry(self.pos - way * i, q + other)
+            return remote(ref, ref, self.xs.at[d, i - 1, q], self.xr.at[d, i - 1, q], self.quad(2))
+
         def start(self):
-            for q in (1, 2, 3):
+            for q in (1, 3, 2):
                 self.first(q).start()
             idx = self.pos * 4 + lane_of(self.xbit, 0)
             self.buf[pl.ds(idx, 1)] = self.src[pl.ds(k, 1)]
-            self.step(0, 0, 0).start()
-            self.step(1, 0, 0).start()
-
-        def enter(self):
-            for q in (1, 2, 3):
-                self.first_arrival(q).wait_recv()
+
+        def enter(self, lanes):
+            for q in lanes:
+                if q:
+                    self.first_arrival(q).wait_recv()
                 self.step(0, 0, q).start()
                 self.step(1, 0, q).start()
 
-        def forward(self, j):
-            for q in range(4):
+        def pass_relays(self, i):
+            for q in (0, 1):
                 for d in (0, 1):
-                    self.arrival(d, j - 1, q).wait_recv()
+                    self.relay(d, i, q).start()
+
+        def forward(self, j, lanes):
+            for q in lanes:
+                for d in (0, 1):
+                    if q > 1 and 0 < self.near == j:
+                        self.relay(d, j, q - 2, 2).wait_recv()
+                    else:
+                        self.arrival(d, j - 1, q).wait_recv()
                     if j < self.h - 1 or d == 0:
                         self.step(d, j, q).start()
 
-        def finish(self):
-            for q in range(4):
+        def finish(self, lanes):
+            for q in lanes:
                 self.arrival(0, self.h - 1, q).wait_recv()
+
+        def finish_near(self):
+            for q in (2, 3):
+                self.first_arrival(q).wait_recv()
+                for i in range(1, self.near):
+                    for d in (0, 1):
+                        self.relay(d, i, q - 2, 2).wait_recv()
 
         def drain(self):
             for q in (1, 2, 3):
@@ -132,18 +164,27 @@
                         self.step(d, j, q).wait_send()
                 return carry
 
-            lax.fori_loop(0, self.h - 1, both, 0)
+            def own(j, carry):
+                for q in (0, 1):
+                    for d in (0, 1):
+                        self.step(d, j, q).wait_send()
+                        self.relay(d, j + 1, q).wait_send()
+                return carry
+
+            if self.near:
+                lax.fori_loop(0, self.near, own, 0)
+            lax.fori_loop(self.near, self.h - 1, both, 0)
             for q in range(4):
                 self.step(0, self.h - 1, q).wait_send()
 
     class Scatter:
-        def __init__(self, part, first, got, qsend, qgot, pos, n, xbit, quad, ring, ss, rs, qs, qr):
+        def __init__(self, part, first, got, qsend, qgot, pos, n, xbit, quad, ring, ss, rs, qs, qr,
+                     near=0, xsend=None, xgot=None, xs=None, xr=None):
             self.__dict__.update(locals())
             self.h = n // 2
 
-        def own(self, d, j, q):
-            ahead = self.h - j if d == 0 else -(self.h - 1 - j)
-            p = (self.pos + sgn * ahead + self.n) % self.n
+        def term(self, d, i, q):
+            p = (self.pos + (sgn * i if d == 0 else -sgn * i) + self.n) % self.n
             return self.part(p, lane_of(self.xbit, q))
 
         def step(self, d, j, q, src):
@@ -153,39 +194,92 @@
         def arrival(self, d, j, q):
             return self.step(d, j, q, self.got.at[d, j, q])
 
+        def hop(self, d, i, q):
+            return remote(self.xsend.at[d, i, q], self.xgot.at[d, i, q], self.xs.at[d, i, q],
+                          self.xr.at[d, i, q], self.quad(2))
+
+        def lanes(self, body, low, high):
+            def lane(q, carry):
+                body(q)
+                return carry
+
+            lax.fori_loop(low, high, lane, 0)
+
         def begin(self):
-            def lane(q, carry):
+            def body(q):
                 for d in (0, 1):
-                    self.first[d, q] = self.own(d, 0, q)
+                    self.first[d, q] = self.term(d, self.h - d, q)
                     self.step(d, 0, q, self.first.at[d, q]).start()
-                return carry
-
-            lax.fori_loop(0, 4, lane, 0)
-
-        def pass_on(self, d, j, q):
-            value = self.own(d, j, q)
+
+            self.lanes(lambda t: body((t + 2) % 4), 0, 4)
+
+        def pass_on(self, d, j, q, hopped=False):
+            i = self.h - d - j
+            value = self.term(d, i, q)
+            if hopped:
+                self.hop(d, i, q).wait_recv()
+                value = value + self.xgot[d, i, q]
             self.arrival(d, j - 1, q).wait_recv()
             self.got[d, j - 1, q] = self.got[d, j - 1, q] + value
             self.step(d, j, q, self.got.at[d, j - 1, q]).start()
 
+        def hop_alone(self, d, i):
+            def body(q):
+                self.xsend[d, i, q] = self.term(d, i, q + 2)
+                self.hop(d, i, q).start()
+
+            self.lanes(body, 0, 2)
+
+        def hop_sum(self, d):
+            i = self.near
+            j = self.h - d - i - 1
+
+            def body(q):
+                value = self.term(d, i, q + 2)
+                self.arrival(d, j, q + 2).wait_recv()
+                self.xsend[d, i, q] = self.got[d, j, q + 2] + value
+                self.hop(d, i, q).start()
+
+            self.lanes(body, 0, 2)
+
         def run(self):
             self.begin()
 
             def both(t, carry):
                 for d in (0, 1):
-                    self.pass_on(d, t // 4 + 1, t % 4)
+                    self.pass_on(d, t // 4 + 1, (t + 2) % 4)
                 return carry
 
             lax.fori_loop(0, 4 * (self.h - 2), both, 0)
-
-            def last(q, carry):
-                self.pass_on(0, self.h - 1, q)
-                return carry
-
-            lax.fori_loop(0, 4, last, 0)
+            self.lanes(lambda t: self.pass_on(0, self.h - 1, (t + 2) % 4), 0, 4)
+
+        def run_near(self):
+            n, h = self.near, self.h
+            self.begin()
+            self.hop_alone(0, 0)
+            self.hop_alone(1, n - 1)
+            for j in range(1, h - 1 - n):
+                for low in (2, 0):
+                    self.lanes(lambda q: [self.pass_on(d, j, q) for d in (0, 1)], low, low + 2)
+            self.hop_alone(0, n - 1)
+            j = h - 1 - n
+            self.hop_sum(1)
+            self.lanes(lambda q: self.pass_on(0, j, q), 2, 4)
+            self.lanes(lambda q: self.pass_on(0, j, q), 0, 2)
+            self.lanes(lambda q: self.pass_on(1, j, q, True), 0, 2)
+            self.hop_sum(0)
+            for i in range(n - 2, 0, -1):
+                self.hop_alone(1, i)
+                self.hop_alone(0, i)
+            for j in range(h - n, h - 1):
+                self.lanes(lambda q: [self.pass_on(d, j, q, True) for d in (1, 0)], 0, 2)
+            self.lanes(lambda q: self.pass_on(0, h - 1, q, True), 0, 2)
 
         def total(self, q):
             value = self.part(self.pos, lane_of(self.xbit, q))
+            if self.near:
+                self.hop(0, 0, q).wait_recv()
+                value = value + self.xgot[0, 0, q]
             self.arrival(1, self.h - 2, q).wait_recv()
             self.arrival(0, self.h - 1, q).wait_recv()
             return value + self.got[0, self.h - 1, q] + self.got[1, self.h - 2, q]
@@ -194,7 +288,7 @@
             return remote(self.qsend.at[i], self.qgot.at[i], self.qs.at[i], self.qr.at[i], self.quad(q))
 
         def finish(self, out):
-            for q in (1, 2, 3):
+            for q in (2, 3, 1):
                 self.qsend[q - 1] = self.total(q)
                 self.handover(q, q - 1).start()
             mine = self.total(0)
@@ -204,33 +298,56 @@
             self.handover(3, 2).wait_recv()
             out[pl.ds(1 - k, 1)] = (self.qgot[0] + self.qgot[2])[None]
 
+        def finish_near(self, out):
+            self.qsend[0] = self.total(1)
+            self.handover(1, 0).start()
+            out[pl.ds(k, 1)] = self.total(0)[None]
+            self.handover(1, 0).wait_recv()
+            out[pl.ds(1 - k, 1)] = self.qgot[pl.ds(0, 1)]
+
         def drain(self):
-            for q in (1, 2, 3):
+            for q in (1, 2, 3) if self.near == 0 else (1,):
                 self.handover(q, q - 1).wait_send()
-
-            def both(t, carry):
-                for d in (0, 1):
-                    self.arrival(d, t // 4, t % 4).wait_send()
-                return carry
-
-            lax.fori_loop(0, 4 * (self.h - 1), both, 0)
-            for q in range(4):
-                self.arrival(0, self.h - 1, q).wait_send()
-
-    halves[0] = feat[:, :BLK]
-    halves[1] = feat[:, BLK:]
+            if self.near:
+                for q in (0, 1):
+                    self.hop(0, 0, q).wait_send()
+                    for d in (0, 1):
+                        for i in range(1, self.near + 1):
+                            self.hop(d, i, q).wait_send()
+            for d in (0, 1):
+                for high, low in ((2, 0), (4, 2)):
+                    last = self.h - d - (self.near if low else 0)
+
+                    def sent(j, carry):
+                        for q in range(low, high):
+                            self.arrival(d, j, q).wait_send()
+                        return carry
+
+                    lax.fori_loop(0, last, sent, 0)
+
+    def split_tiles(g, src):
+        def one(s, carry):
+            high, low = split(src[s])
+            pairs[g * slots + s] = jnp.concatenate([high, low], axis=1)
+            return carry
+
+        lax.fori_loop(0, slots, one, 0)
+
+    def product(pair, block):
+        high, low = split(block)
+        right = jnp.concatenate([jnp.concatenate([high, high], axis=0),
+                                 jnp.concatenate([low, jnp.zeros_like(low)], axis=0)], axis=1)
+        both = jnp.dot(pair, right, preferred_element_type=F32)
+        return both[:, :BLK] + both[:, BLK:]
+
     column = Gather(xb, halves, y, ny, xh, quad_x, at_y, xq_s, xq_r, xr_s, xr_r)
     column.start()
     send_rows = remote(trows, meta_out.at[0], tq_s.at[1], tq_r.at[1], quad_x(1))
     send_cols = remote(tcols, meta_out.at[1], tq_s.at[2], tq_r.at[2], quad_x(1))
     send_rows.start()
     send_cols.start()
-    own_rows = pltpu.make_async_copy(trows, sm.at[0], mloc.at[0])
-    own_cols = pltpu.make_async_copy(tcols, sm.at[1], mloc.at[1])
-    own_rows.start()
-    own_cols.start()
-    column.enter()
-    send_tiles = remote(tiles, sib, tq_s.at[0], tq_r.at[0], quad_x(1))
+    send_tiles = remote(tiles_in, sib, tq_s.at[0], tq_r.at[0], quad_x(1))
+    column.enter((0, 1))
     send_tiles.start()
     send_rows.wait_recv()
     send_cols.wait_recv()
@@ -242,12 +359,18 @@
     sib_cols.start()
     sib_rows.wait()
     sib_cols.wait()
-    for j in range(1, ny // 2):
-        column.forward(j)
+    column.forward(1, (0, 1))
+    column.enter((2, 3))
+    load[2].wait()
+    split_tiles(0, tiles)
+    for j in range(2, ny // 2):
+        column.forward(j, (0, 1))
+        column.forward(j - 1, (2, 3))
     send_tiles.wait_recv()
-    column.finish()
-
-    tile_of = (tiles, sib)
+    split_tiles(1, sib)
+    column.finish((0, 1))
+    column.forward(ny // 2 - 1, (2, 3))
+    column.finish((2, 3))
 
     def row_at(g, s):
         return sm[2 * g, s]
@@ -262,7 +385,7 @@
         for g in (0, 1):
             col = col_at(g, s)
             place = (col % ny) * 4 + (col // ny) * 2 + core_of(g)
-            prod[g * slots + s] = dot3(tile_of[g][s], xb[place])
+            prod[g * slots + s] = product(pairs[g * slots + s], xb[place])
         return carry
 
     lax.fori_loop(0, slots, products, 0)
@@ -275,10 +398,13 @@
                 acc = acc + jnp.where(row_at(g, s) == block, 1.0, 0.0) * prod[g * slots + s]
         return acc
 
-    rows = Scatter(row_part, zs, zr, zqs, zqr, z, nz, xl, quad_l, at_z, zrs_s, zrs_r, zq_s, zq_r)
-    rows.run()
-    rows.finish(agg)
-
+    rows = Scatter(row_part, zs, zr, zqs, zqr, z, nz, xl, quad_l, at_z, zrs_s, zrs_r, zq_s, zq_r,
+                   NEAR, hs, hr, hop_s, hop_r)
+    rows.run_near()
+    rows.finish_near(agg)
+
+    load[3].wait()
+    load[4].wait()
     aggregated = jnp.concatenate([agg[0], agg[1]], axis=1)
     hidden = jnp.tanh(dot3(aggregated, w[...]))
     hid[...] = hidden
@@ -287,8 +413,16 @@
     column.drain()
     halves[0] = back[:, :BLK]
     halves[1] = back[:, BLK:]
-    group = Gather(ab, halves, z, nz, xl, quad_l, at_z, bq_s, bq_r, br_s, br_r)
+    group = Gather(ab, halves, z, nz, xl, quad_l, at_z, bq_s, bq_r, br_s, br_r, NEAR, bx_s, bx_r)
     group.start()
+
+    def turn_tiles(g, src):
+        def one(s, carry):
+            high, low = split(src[s].T)
+            pairs[g * slots + s] = jnp.concatenate([high, low], axis=1)
+            return carry
+
+        lax.fori_loop(0, slots, one, 0)
 
     g0[...] = dot3(aggregated, delta, ((0,), (0,))).reshape(g0.shape)
     m = lane_of(xl, 0)
@@ -322,9 +456,11 @@
 
     for d in range(1, ny):
         sum_y(d).start()
-    group.enter()
-
-    group.forward(1)
+    group.enter((0, 1))
+
+    group.forward(1, (0, 1))
+    group.pass_relays(1)
+    turn_tiles(0, tiles)
     acc = g0[chunk(y)]
     for d in range(1, ny):
         sum_y(d).wait_recv()
@@ -333,7 +469,8 @@
     for q in (1, 2, 3):
         sum_quad(q).start()
 
-    group.forward(2)
+    group.forward(2, (0, 1))
+    turn_tiles(1, sib)
     acc = s1[m]
     for q in (1, 2, 3):
         sum_quad(q).wait_recv()
@@ -341,14 +478,17 @@
     s2[...] = acc
     sum_x().start()
 
-    group.forward(3)
+    group.forward(3, (0, 1))
+    group.pass_relays(3)
+    group.pass_relays(2)
     sum_x().wait_recv()
     s4[0] = s2[...] + r3[...]
     for d in range(1, nz):
         sum_z(d).start()
     r4[z] = s4[0]
 
-    group.forward(4)
+    group.forward(4, (0, 1))
+    group.forward(3, (2, 3))
     for d in range(1, nz):
         sum_z_in(d).wait_recv()
     acc = r4[0]
@@ -358,18 +498,21 @@
     for q in (1, 2, 3):
         spread_quad(q, 0).start()
 
-    for j in range(5, nz // 2):
-        group.forward(j)
+    group.forward(5, (0, 1))
+    group.forward(4, (2, 3))
     for q in (1, 2, 3):
         spread_quad(q, q).wait_recv()
     for d in range(1, ny):
         spread_y(d, 0).start()
-    group.finish()
+    group.finish((0, 1))
+    group.forward(5, (2, 3))
+    group.finish((2, 3))
+    group.finish_near()
 
     def back_products(s, carry):
         for g in (0, 1):
             row = jnp.maximum(row_at(g, s), 0)
-            prod[g * slots + s] = dot3(tile_of[g][s], ab[row], ((0,), (0,)))
+            prod[g * slots + s] = product(pairs[g * slots + s], ab[row])
         return carry
 
     lax.fori_loop(0, slots, back_products, 0)
@@ -423,8 +566,9 @@
     dma = pltpu.SemaphoreType.DMA
     vmem = pltpu.VMEM
     scratch = [
-        vmem((2,) + half, F32), vmem((ny * 4,) + half, F32), vmem((slots,) + half, F32),
-        vmem((8, 128), jnp.int32), vmem((2 * slots,) + half, F32),
+        vmem((2,) + half, F32), vmem((width, width), F32), vmem((node_count, width), F32),
+        vmem((slots,) + half, F32), vmem((ny * 4,) + half, F32), vmem((slots,) + half, F32),
+        vmem((2 * slots,) + half, F32),
         vmem((2, 4) + half, F32), vmem((2, hz, 4) + half, F32), vmem((3,) + half, F32), vmem((3,) + half, F32),
         vmem((2,) + half, F32), vmem((nz * 4,) + half, F32),
         vmem((2, 4) + half, F32), vmem((2, hy, 4) + half, F32), vmem((3,) + half, F32), vmem((3,) + half, F32),
@@ -433,15 +577,19 @@
         vmem((3, 8, width), F32), vmem((8, width), F32), vmem((8, width), F32),
         vmem((nz, 8, width), F32), vmem((1, 8, width), F32), vmem((lines, 8, width), F32),
         pltpu.SMEM((4, slots), jnp.int32), dma((4,)), dma((3,)), dma((3,)),
+        dma((5,)),
         dma((3,)), dma((3,)), dma((2, hy, 4)), dma((2, hy, 4)),
         dma((2, hz, 4)), dma((2, hz, 4)), dma((3,)), dma((3,)),
         dma((3,)), dma((3,)), dma((2, hz, 4)), dma((2, hz, 4)),
         dma((2, hy, 4)), dma((2, hy, 4)), dma((3,)), dma((3,)),
         dma((ny - 1,)), dma((ny - 1,)), dma((3,)), dma((3,)), dma((1,)), dma((1,)),
         dma((nz - 1,)), dma((nz - 1,)), dma((3,)), dma((3,)), dma((ny - 1,)), dma((ny - 1,)),
+        vmem((2, NEAR + 1, 2) + half, F32), vmem((2, NEAR + 1, 2) + half, F32),
+        dma((2, NEAR + 1, 2)), dma((2, NEAR + 1, 2)), dma((2, NEAR, 2)), dma((2, NEAR, 2)),
+        vmem((2 * slots, BLK, 2 * BLK), BF16),
     ]
     in_vmem = pl.BlockSpec(memory_space=pltpu.VMEM)
-    anywhere = pl.BlockSpec(memory_space=pl.ANY)
+    in_hbm = pl.BlockSpec(memory_space=pltpu.HBM)
     out = pl.pallas_call(
         functools.partial(layer_kernel, ny, nz),
         out_shape=(
@@ -450,11 +598,11 @@
             jax.ShapeDtypeStruct((width, width), F32),
             jax.ShapeDtypeStruct((2, slots), jnp.int32),
         ),
-        in_specs=[in_vmem] * 4 + [anywhere] * 2,
-        out_specs=(in_vmem, in_vmem, in_vmem, anywhere),
+        in_specs=[in_hbm] * 6,
+        out_specs=(in_vmem, in_vmem, in_vmem, in_hbm),
         scratch_shapes=scratch,
         compiler_params=pltpu.CompilerParams(
-            collective_id=0, has_side_effects=True, vmem_limit_bytes=40 * 1024 * 1024),
+            collective_id=0, has_side_effects=True, vmem_limit_bytes=62 * 1024 * 1024),
     )(features, weight, cotangent, tiles[0, 0], tile_rows[0, 0], tile_cols[0, 0])
     return out[0], out[1], out[2]
 

time: 162 us -> 152 us (0.938)
  Pallas kernels: 155 us -> 148 us
  local copies, waits for them, and re-layouts: 6.65 us -> 2.98 us
    pallas_call x1, Pallas kernels: 155 us -> 148 us  [on_device(): pl.pallas_call(functools.partial(layer_kernel, ny, nz), out_shape=(jax.Sh...]
    unnamed x15 -> x7, local copies, waits for them, and re-layouts: 6.65 us -> 2.98 us
where the time goes in v2:
time: 152 us
  Pallas kernels  148 us (97%)
  local copies, waits for them, and re-layouts  2.98 us (2%)
    pallas_call x1, Pallas kernels, on_device(): pl.pallas_call(functools.partial(layer_kernel, ny, nz), out_shape=(jax.Sh...  148 us

profile of v2, /device:TPU:1, one launch (start us, length us, event | category | flops | bytes accessed | tf_op | source)
XLA Modules:
  0.0 152.0 jit_solution(11400694417680124561)
XLA Ops:
  0.6 148.4 %shard_map.85 = (f32[128,256]{1,0:T(8,128)}, f32[128,256]{1,0:T(8,128)}, f32[256,256]{1,0:T(8,128)}, s32[2,16]{1,0:T(2,128)}) custom-call(f32[128,256]{1,0:T(8,128)} %feat.1, f32[256,256]{1,0:T(8,128)} %w_in.1, f32[128,256]{1,0:T(8,128)} %cot_in.1, f32[16,128,128]{2,1,0:T(8,128)} %bitcast.3, s32[16]{0:T(128)} %bitcast.4, s32[16]{0:T(128)} %bitcast.5), custom_call_target="tpu_custom_call" | custom-call | tf_op jit(solution)/shard_map/pallas_call | solution.py:593
  149.0 0.0 copy-start.1
  149.0 0.0 copy-start
  149.1 1.6 %copy.12 = f32[128,256]{1,0:T(8,128)} copy(f32[128,256]{1,0:T(8,128)} %get-tuple-element.12) | data formatting | bytes 262144
  150.7 0.0 copy-done.1
  150.7 0.7 copy.13
  151.3 0.0 copy-done
  151.3 0.7 copy.14
Async XLA Ops:
  149.0 1.6 %copy-start.1 = (f32[128,256]{1,0:T(8,128)S(1)}, f32[128,256]{1,0:T(8,128)}, u32[]{:S(2)}) copy-start(f32[128,256]{1,0:T(8,128)} %get-tuple-element.13) | copy-start | bytes 393220
  149.0 2.3 %copy-start = (f32[256,256]{1,0:T(8,128)S(1)}, f32[256,256]{1,0:T(8,128)}, u32[]{:S(2)}) copy-start(f32[256,256]{1,0:T(8,128)} %get-tuple-element.14) | copy-start | bytes 786436
